TPU v7x, 128 devices: a whole 4x4x4 slice. The times are simulated.
128 devices in a mesh: row: 16 (over y, z), col: 8 (over x, core).
Axes of the slice: x: 4, y: 4, z: 4, core: 2. Of those that a mesh axis runs over, the one named last changes fastest.
Arguments:
- solved: bfloat16 [8192, 16384], P('col', 'row'), may hold values from -6 to 6
- factor_rows: bfloat16 [1024, 8192], P(None, 'col'), may hold values from -0.0625 to 0.0625
- diag_inverse: bfloat16 [1024, 1024], replicated, may hold values from -1 to 1, as said below
- features: bfloat16 [16384, 1024], P('row'), may hold values from -6 to 6
- covariance: float32 [16384, 16384], P('row', 'col'), may hold values from -6 to 6
Outputs:
- cov_out: float32 [16384, 16384], P('row', 'col')
Inputs may be any that keep to these rules, and one draw needn't show every extreme that they name: diag_inverse is lower triangular; its diagonal lies between 1 / sqrt(1024) and 3 / sqrt(1024).
All inputs are finite; a program needn't handle non-finite values.
Results may differ from a plain program's by a relative error of at most 0.0018.
Values may be sent and summed in bfloat16 or wider, within the bound.
A program may use at most 128 MiB of HBM per device.

v0:
```python
import jax
import jax.numpy as jnp
from jax import lax
from jax.sharding import PartitionSpec as P


def broadcast(value, axis, root):
    mine = lax.axis_index(axis) == root
    return lax.psum(jnp.where(mine, value, jnp.zeros_like(value)), axis)


def apply_inverse(residual, diag_inverse):
    product = lax.dot_general(
        residual, diag_inverse, (((1,), (1,)), ((), ())), preferred_element_type=jnp.float32
    )
    return product.astype(jnp.bfloat16)


def body(solved, factor_rows, diag_inverse, features, covariance):
    partial_value = lax.dot_general(
        solved, factor_rows, (((0,), (1,)), ((), ())), preferred_element_type=jnp.float32
    )
    shared = lax.psum_scatter(partial_value, "col", scatter_dimension=0, tiled=True)
    count_rows = shared.shape[0]
    own_features = lax.dynamic_slice_in_dim(
        features, lax.axis_index("col") * count_rows, count_rows, 0
    )
    residual = (own_features.astype(jnp.float32) - shared).astype(jnp.bfloat16)
    row_panel = lax.all_gather(apply_inverse(residual, diag_inverse), "col", axis=0, tiled=True)
    groups = lax.axis_size("row") // lax.axis_size("col")
    column = lax.axis_index("col")
    blocks = []
    for member in range(groups):
        blocks.append(broadcast(row_panel, "row", column * groups + member))
    col_panel = jnp.concatenate(blocks, 0)
    update = lax.dot_general(
        row_panel, col_panel, (((1,), (1,)), ((), ())), preferred_element_type=jnp.float32
    )
    return covariance + update


def solution(mesh):
    placed = (P("col", "row"), P(None, "col"), P(), P("row", None), P("row", "col"))
    return jax.shard_map(
        body, mesh=mesh, in_specs=placed, out_specs=P("row", "col"), check_vma=False
    )
```

profile of v0, /device:TPU:1, one launch (start us, length us, event | category | flops | bytes accessed | tf_op | source)
XLA Modules:
  0.0 210.6 jit_solution(5080284841531963946)
XLA Ops:
  6.5 0.0 copy-start
  6.5 0.0 reduce-scatter.2.cloned.1.call-start
  6.5 1.6 copy-done
  8.1 6.0 %fusion.10 = f32[1024,1024]{1,0:T(8,128)} fusion(bf16[1024,1024]{1,0:T(8,128)(2,1)S(1)} %copy-done, bf16[1024,1024]{1,0:T(8,128)(2,1)} %param.6), kind=kOutput, calls=%fused_computation.12 | convolution fusion | flops 2147483648 | bytes 8388608 | tf_op jit(solution)/shard_map/dot_general | solution.py:20
  14.1 0.0 reduce-scatter.2.cloned.1.call-update
  14.1 0.0 all-gather.2.cloned.1.call-start
  14.2 38.2 %reduce-scatter.2.cloned.1.call-done = f32[128,1024]{1,0:T(8,128)} async-done(((f32[1024,1024]{1,0:T(8,128)}), f32[128,1024]{1,0:T(8,128)}) %reduce-scatter.2.cloned.1.call-update) | async-done | bytes 524304 | tf_op jit(solution)/shard_map/reduce_scatter | solution.py:23
  52.3 3.4 %convolution_convert_fusion = bf16[128,1024]{1,0:T(8,128)(2,1)} fusion(bf16[1024,1024]{1,0:T(8,128)(2,1)} %param.7, f32[128,1024]{1,0:T(8,128)} %reduce-scatter.2.cloned.1.call-done, bf16[1024,1024]{1,0:T(8,128)(2,1)} %param.8, s32[]{:T(128)S(6)} %select_n.17), kind=kOutput, calls=%fused_computation.7 | convolution fusion | flops 268959744 | bytes 3145732 | tf_op jit(solution)/shard_map/dot_general | solution.py:13
  55.7 0.0 all-gather.2.cloned.1.call-update
  55.8 0.0 all-reduce.3.cloned.1.call-start
  55.8 27.5 %all-gather.2.cloned.1.call-done = bf16[1024,1024]{1,0:T(8,128)(2,1)} async-done(((bf16[128,1024]{1,0:T(8,128)(2,1)}), bf16[1024,1024]{1,0:T(8,128)(2,1)}) %all-gather.2.cloned.1.call-update) | async-done | bytes 2097168 | tf_op jit(solution)/shard_map/all_gather | solution.py:29
  83.3 3.9 %broadcast_select_fusion.1 = (bf16[1024,1024]{1,0:T(8,128)(2,1)}, bf16[1024,1024]{1,0:T(8,128)(2,1)}) fusion(bf16[1024,1024]{1,0:T(8,128)(2,1)} %all-gather.2.cloned.1.call-done, pred[]{:T(512)S(6)} %eq.6, pred[]{:T(512)S(6)} %eq.7), kind=kLoop, calls=%fused_computation.6 | loop fusion | flops 2097152 | bytes 6291458 | tf_op jit(solution)/shard_map/jit(_where)/select_n | solution.py:9
  87.2 0.0 all-reduce.3.cloned.1.call-update
  87.3 103.7 %all-reduce.3.cloned.1.call-done = (bf16[1024,1024]{1,0:T(8,128)(2,1)}, bf16[1024,1024]{1,0:T(8,128)(2,1)}) async-done(((bf16[1024,1024]{1,0:T(8,128)(2,1)}, bf16[1024,1024]{1,0:T(8,128)(2,1)}), (bf16[1024,1024]{1,0:T(8,128)(2,1)}, bf16[1024,1024]{1,0:T(8,128)(2,1)})) %all-reduce.3.cloned.1.call-update) | async-done | bytes 4194320 | tf_op jit(solution)/shard_map/psum | solution.py:9
  190.9 13.2 %fusion.4 = f32[1024,2048]{1,0:T(8,128)} fusion(f32[1024,2048]{1,0:T(8,128)} %param.9, bf16[1024,1024]{1,0:T(8,128)(2,1)} %all-gather.2.cloned.1.call-done, bf16[1024,1024]{1,0:T(8,128)(2,1)} %get-tuple-element.5, bf16[1024,1024]{1,0:T(8,128)(2,1)} %get-tuple-element.6), kind=kOutput, calls=%fused_computation.4 | convolution fusion | flops 4305453056 | bytes 23068672 | tf_op jit(solution)/shard_map/dot_general | solution.py:36
Async XLA Ops:
  6.5 1.6 copy-start
  6.5 45.8 %reduce-scatter.2.cloned.1.call-start = ((), (), s32[]{:S(2)}) async-start(), calls=%async_computation.1 | async-start | bytes 4718592 | tf_op jit(solution)/shard_map/reduce_scatter | solution.py:23
  14.1 69.2 %all-gather.2.cloned.1.call-start = ((), (), s32[]{:S(2)}) async-start(), calls=%async_computation.2 | async-start | bytes 2359296 | tf_op jit(solution)/shard_map/all_gather | solution.py:29
  55.8 135.2 %all-reduce.3.cloned.1.call-start = ((), (), s32[]{:S(2)}) async-start(), calls=%async_computation.3 | async-start | bytes 8388608 | tf_op jit(solution)/shard_map/psum | solution.py:9
Sparse Core Ops, SparseCore 0:
  14.3 38.0 reduce-scatter.1
  55.9 27.4 all-gather.1
  87.4 103.4 all-reduce.2
where the time goes:
time: 211 us
  waiting for transfers between devices  169 us (80%)
  matrix products  22.6 us (11%)
  between operations  13.1 us (6%)
  other arithmetic  3.91 us (2%)
    psum x1, waiting for transfers between devices, broadcast(): return lax.psum(jnp.where(mine, value, jnp.zeros_like(value)), axis)  104 us
    reduce_scatter x1, waiting for transfers between devices, body(): lax.psum_scatter(partial_value, 'col', scatter_dimension=0, tiled=True)  38.2 us
    all_gather x1, waiting for transfers between devices, body(): lax.all_gather(apply_inverse(residual, diag_inverse), 'col', axis=0, tile...  27.5 us
    dot_general x1, matrix products, body(): lax.dot_general(row_panel, col_panel, (((1,), (1,)), ((), ())), preferred...  13.2 us
    dot_general x1, matrix products, body(): lax.dot_general(solved, factor_rows, (((0,), (1,)), ((), ())), preferred_...  5.98 us
  transfers between devices with their start and end apart: 3, of which 3 were waited for; matrix products, arithmetic and copies ran while one was open for 0% of the time, Pallas kernels for 0%

commit v1 on v0

v1 whole, which is shorter than its diff:
```python
import jax
import jax.numpy as jnp
from jax import lax
from jax.experimental import pallas as pl
from jax.experimental.pallas import tpu as pltpu
from jax.sharding import PartitionSpec as P

F32 = jnp.float32
BF16 = jnp.bfloat16
CHUNKS = 4
KB = 256
NT = (((1,), (1,)), ((), ()))

ORDERS = (13882568, 2178540, 6835325, 16075976, 10973347, 2185148, 2189180, 10973347, 14592200, 4579820, 5801852, 14592088, 16114952, 7052332, 8217132, 16373000)
LOW = (22442, 1536, 0, 128, 56512, 1088, 8192, 41472, 56366, 5126, 2, 36994, 2798, 117, 1, 34848)
HIGH = (8, 55267, 1808, 256, 32769, 55565, 278, 12288, 6192, 53412, 4100, 4128, 2817, 2156, 68, 48)


def pick(table, role):
    value = jnp.int32(table[0])
    for index in range(1, len(table)):
        value = jnp.where(role == index, jnp.int32(table[index]), value)
    return value


def kernel(
    solved, factor, dinv, features, covariance, acc,
    sv, fv, dv, fe, res, own, sib_out, sib_in, red_out, red_in, row_panel, col_panel,
    load_sem, sv_sem, sib_s, sib_r, red_s, red_r, gat_s, gat_r, tree_s, tree_r,
):
    row = lax.axis_index("row")
    col = lax.axis_index("col")
    y, z = row // 4, row % 4
    x, core = col // 2, col % 2

    def at(xx, yy, zz, cc):
        return {"row": ((yy + 4) % 4) * 4 + (zz + 4) % 4, "col": ((xx + 4) % 4) * 2 + cc}

    sibling = at(x, y, z, 1 - core)
    x_next, x_prev = at(x + 1, y, z, core), at(x - 1, y, z, core)
    around = (at(x, y + 1, z, core), at(x, y - 1, z, core), at(x, y, z + 1, core), at(x, y, z - 1, core))

    role = ((y - x + 4) % 4) * 4 + (z - 2 * core + 4) % 4
    order, low, high = pick(ORDERS, role), pick(LOW, role), pick(HIGH, role)
    is_source = role < 2

    def remote(src, dst, send, recv, device):
        return pltpu.make_async_remote_copy(
            src_ref=src, dst_ref=dst, send_sem=send, recv_sem=recv,
            device_id=device, device_id_type=pl.DeviceIdType.MESH,
        )

    def frames_of(place):
        chip = (x + place % 4) % 4
        half = core if place < 4 else 1 - core
        return pl.multiple_of(chip * 256 + half * 128, 128)

    def sv_load(place):
        return pltpu.make_async_copy(
            solved.at[:, pl.ds(frames_of(place), 128)], sv.at[:, pl.ds(place * 128, 128)], sv_sem.at[place]
        )

    fv_loads = [
        pltpu.make_async_copy(factor.at[pl.ds(k * KB, KB)], fv.at[pl.ds(k * KB, KB)], load_sem.at[k])
        for k in range(CHUNKS)
    ]
    fe_load = pltpu.make_async_copy(features.at[pl.ds(frames_of(0), 128)], fe, load_sem.at[4])
    dv_load = pltpu.make_async_copy(dinv, dv, load_sem.at[5])
    acc_load = pltpu.make_async_copy(covariance, acc, load_sem.at[6])

    fv_loads[0].start()
    for place in (4, 5, 6, 7, 0, 1, 2, 3):
        sv_load(place).start()
    for k in range(1, CHUNKS):
        fv_loads[k].start()
    fe_load.start()
    dv_load.start()
    acc_load.start()

    barrier = pltpu.get_barrier_semaphore()
    for device in (sibling, x_next, x_prev) + around:
        pl.semaphore_signal(barrier, inc=1, device_id=device, device_id_type=pl.DeviceIdType.MESH)

    def rows_of(k):
        return pl.ds(pl.multiple_of(k * KB, KB), KB)

    def sib_copy(k):
        return remote(sib_out.at[k], sib_in.at[k], sib_s.at[k], sib_r.at[k], sibling)

    def red_copy(k, m):
        return remote(
            red_out.at[k, m], red_in.at[k, m], red_s.at[k, m], red_r.at[k, m], x_next if m % 2 == 0 else x_prev
        )

    def partial_sibling(k):
        sib_out[k] = jnp.dot(fv[rows_of(k), :], sv[:, 512:], preferred_element_type=F32).astype(BF16)

    def partial_own(k):
        own[k] = jnp.dot(fv[rows_of(k), :], sv[:, :512], preferred_element_type=F32)

    def reduce_start(k):
        sib_copy(k).wait_recv()
        total = own[k] + sib_in[k].astype(F32)
        own[k] = total
        red_out[k, 0] = total[:128, 256:384].astype(BF16)
        red_out[k, 1] = total[128:, 256:384].astype(BF16)
        red_copy(k, 0).start()
        red_copy(k, 1).start()
        red_out[k, 2] = total[128:, 128:256].astype(BF16)
        red_out[k, 3] = total[:128, 384:].astype(BF16)
        red_copy(k, 2).start()
        red_copy(k, 3).start()

    def reduce_merge(k):
        red_copy(k, 0).wait_recv()
        red_out[k, 4] = (own[k, :128, 128:256] + red_in[k, 0].astype(F32)).astype(BF16)
        red_copy(k, 4).start()
        red_copy(k, 1).wait_recv()
        red_out[k, 5] = (own[k, 128:, 384:] + red_in[k, 1].astype(F32)).astype(BF16)
        red_copy(k, 5).start()

    def piece(k, chip, half, offset=0, size=128):
        first = pl.multiple_of(((chip + 4) % 4) * 256 + half * 128 + offset, 64)
        return row_panel.at[k, pl.ds(first, size)]

    def gather_copy(k, m):
        ref = (
            lambda: piece(k, x, core),
            lambda: piece(k, x, core),
            lambda: piece(k, x - 1, core, 0, 64),
            lambda: piece(k, x + 1, core, 64, 64),
            lambda: piece(k, x, core),
            lambda: piece(k, x - 1, core),
            lambda: piece(k, x + 1, core),
            lambda: piece(k, x + 2, core),
        )[m]()
        device = (x_next, x_prev, x_next, x_prev, sibling, sibling, sibling, sibling)[m]
        return remote(ref, ref, gat_s.at[k, m], gat_r.at[k, m], device)

    def unit(k, u):
        return col_panel.at[k, u]

    def own_unit(k, j):
        @pl.when(is_source)
        def _():
            first = pl.multiple_of(((x + j) % 4) * 256, 256)
            pltpu.make_async_copy(
                row_panel.at[k, pl.ds(first, 256)], unit(k, role * 4 + j), tree_r.at[k, role * 4 + j]
            ).start()

    def make_panel(k):
        for m in (2, 3, 4, 5):
            red_copy(k, m).wait_recv()
        top = own[k, :128, :128] + red_in[k, 4].astype(F32) + red_in[k, 3].astype(F32)
        bottom = own[k, 128:, :128] + red_in[k, 5].astype(F32) + red_in[k, 2].astype(F32)
        summed = jnp.concatenate([top.T, bottom.T], axis=1)
        cols = pl.ds(pl.multiple_of(k * KB, KB), KB)
        res[:, cols] = (fe[:, cols].astype(F32) - summed).astype(BF16)
        panel = lax.dot_general(res[...], dv[rows_of(k), :], NT, preferred_element_type=F32).astype(BF16)
        first = pl.multiple_of(x * 256 + core * 128, 128)
        row_panel[k, pl.ds(first, 128)] = panel
        gather_copy(k, 0).start()
        gather_copy(k, 1).start()
        gather_copy(k, 4).start()

    def gather_pass(k):
        gather_copy(k, 0).wait_recv()
        gather_copy(k, 2).start()
        gather_copy(k, 5).start()
        gather_copy(k, 1).wait_recv()
        gather_copy(k, 3).start()
        gather_copy(k, 6).start()
        gather_copy(k, 4).wait_recv()
        own_unit(k, 0)

    def gather_opposite(k):
        gather_copy(k, 2).wait_recv()
        gather_copy(k, 3).wait_recv()
        gather_copy(k, 7).start()
        gather_copy(k, 5).wait_recv()
        own_unit(k, 3)
        gather_copy(k, 6).wait_recv()
        own_unit(k, 1)

    def gather_end(k):
        gather_copy(k, 7).wait_recv()
        own_unit(k, 2)

    res[...] = jnp.zeros_like(res)
    fv_loads[0].wait()
    for place in (4, 5, 6, 7):
        sv_load(place).wait()
    partial_sibling(0)
    pl.semaphore_wait(barrier, 7)
    sib_copy(0).start()
    for place in (0, 1, 2, 3):
        sv_load(place).wait()
    partial_own(0)
    reduce_start(0)
    fv_loads[1].wait()
    partial_sibling(1)
    sib_copy(1).start()
    partial_own(1)
    reduce_merge(0)
    fv_loads[2].wait()
    partial_sibling(2)
    sib_copy(2).start()
    partial_own(2)
    fe_load.wait()
    dv_load.wait()
    make_panel(0)
    reduce_start(1)
    fv_loads[3].wait()
    partial_sibling(3)
    sib_copy(3).start()
    gather_pass(0)
    partial_own(3)
    reduce_merge(1)
    gather_opposite(0)
    gather_end(0)
    acc_load.wait()

    def tree_copy(k, u, d):
        return remote(unit(k, u), unit(k, u), tree_s.at[k, u, d], tree_r.at[k, u], around[d])

    def passes(u, d):
        word = jnp.where(u < 4, low, high)
        place = (u % 4) * 4 + d
        return (lax.shift_right_logical(word, place) & 1) == 1

    @pl.loop(0, CHUNKS * 8)
    def _(t):
        k, i = t // 8, t % 8
        for stage, when, ahead in (
            (make_panel, 0, 1), (reduce_start, 1, 2), (gather_pass, 2, 1), (reduce_merge, 3, 2),
            (gather_opposite, 5, 1), (gather_end, 7, 1),
        ):
            @pl.when(jnp.logical_and(i == when, k + ahead < CHUNKS))
            def _():
                stage(k + ahead)

        u = lax.shift_right_logical(order, 3 * i) & 7
        tree_copy(k, u, 0).wait_recv()
        for d in range(4):
            @pl.when(passes(u, d))
            def _():
                tree_copy(k, u, d).start()
        first = pl.multiple_of((u // 4) * 1024 + ((x + u % 4) % 4) * 256, 256)
        acc[:, pl.ds(first, 256)] += lax.dot_general(
            row_panel[k], col_panel[k, u], NT, preferred_element_type=F32
        )

    @pl.loop(0, CHUNKS * 8)
    def _(t):
        k, u = t // 8, t % 8
        for d in range(4):
            @pl.when(passes(u, d))
            def _():
                tree_copy(k, u, d).wait_send()

    @pl.loop(0, CHUNKS)
    def _(k):
        sib_copy(k).wait_send()
        for m in range(6):
            red_copy(k, m).wait_send()
        for m in range(8):
            gather_copy(k, m).wait_send()


def body(solved, factor_rows, diag_inverse, features, covariance):
    any_place = pl.BlockSpec(memory_space=pl.ANY)
    dma = pltpu.SemaphoreType.DMA
    return pl.pallas_call(
        kernel,
        out_shape=pltpu.VMEM((1024, 2048), F32),
        in_specs=[any_place] * 5,
        out_specs=pl.BlockSpec(memory_space=pltpu.VMEM),
        scratch_shapes=[
            pltpu.VMEM((1024, 1024), BF16),
            pltpu.VMEM((1024, 1024), BF16),
            pltpu.VMEM((1024, 1024), BF16),
            pltpu.VMEM((128, 1024), BF16),
            pltpu.VMEM((128, 1024), BF16),
            pltpu.VMEM((CHUNKS, KB, 512), F32),
            pltpu.VMEM((CHUNKS, KB, 512), BF16),
            pltpu.VMEM((CHUNKS, KB, 512), BF16),
            pltpu.VMEM((CHUNKS, 6, 128, 128), BF16),
            pltpu.VMEM((CHUNKS, 6, 128, 128), BF16),
            pltpu.VMEM((CHUNKS, 1024, KB), BF16),
            pltpu.VMEM((CHUNKS, 8, 256, KB), BF16),
            dma((7,)),
            dma((8,)),
            dma((CHUNKS,)),
            dma((CHUNKS,)),
            dma((CHUNKS, 6)),
            dma((CHUNKS, 6)),
            dma((CHUNKS, 8)),
            dma((CHUNKS, 8)),
            dma((CHUNKS, 8, 4)),
            dma((CHUNKS, 8)),
        ],
        compiler_params=pltpu.CompilerParams(
            collective_id=0, has_side_effects=True, vmem_limit_bytes=44 * 2**20
        ),
        cost_estimate=pl.CostEstimate(flops=7 * 10**9, bytes_accessed=24 * 10**6, transcendentals=0),
    )(solved, factor_rows, diag_inverse, features, covariance)


def solution(mesh):
    placed = (P("col", "row"), P(None, "col"), P(), P("row", None), P("row", "col"))
    return jax.shard_map(
        body, mesh=mesh, in_specs=placed, out_specs=P("row", "col"), check_vma=False
    )
```

time: 211 us -> 127 us (0.60)
  the two profiles are of different devices: /device:TPU:1 before, /device:TPU:49 now
where the time goes in v1:
time: 127 us
  Pallas kernels  124 us (98%)
  local copies, waits for them, and re-layouts  3.4 us (3%)
    pallas_call x1, Pallas kernels, body(): pl.pallas_call(kernel, out_shape=pltpu.VMEM((1024, 2048), F32), in_specs=...  124 us
    unnamed x1, local copies, waits for them, and re-layouts  3.4 us

profile of v1, /device:TPU:49, one launch (start us, length us, event | category | flops | bytes accessed | tf_op | source)
XLA Modules:
  0.0 127.3 jit_solution(14589190741554349279)
XLA Ops:
  0.0 123.9 %shard_map.55 = f32[1024,2048]{1,0:T(8,128)S(1)} custom-call(bf16[1024,1024]{1,0:T(8,128)(2,1)} %solved.1, bf16[1024,1024]{1,0:T(8,128)(2,1)} %factor.1, bf16[1024,1024]{1,0:T(8,128)(2,1)} %dinv.1, bf16[1024,1024]{1,0:T(8,128)(2,1)} %features.1, f32[1024,2048]{1,0:T(8,128)} %covariance.1), custom_call_target="tpu_custom_call" | custom-call | flops 7000000000 | bytes 24000000 | tf_op jit(solution)/shard_map/pallas_call | solution.py:273
  123.9 3.4 %copy.7 = f32[1024,2048]{1,0:T(8,128)} copy(f32[1024,2048]{1,0:T(8,128)S(1)} %shard_map.55) | data formatting | bytes 16777216

commit v2 on v0

v2 whole, which is shorter than its diff:
```python
import jax
import jax.numpy as jnp
from jax import lax
from jax.experimental import pallas as pl
from jax.experimental.pallas import tpu as pltpu
from jax.sharding import PartitionSpec as P

F32 = jnp.float32
BF16 = jnp.bfloat16
CHUNKS = 4
KB = 256
NT = (((1,), (1,)), ((), ()))
MESH = pl.DeviceIdType.MESH

(
    PART_SIBLING, PART_OWN, REDUCE, PANEL, FROM_PREV, FROM_NEXT, FROM_OPPOSITE, ROW_DONE,
) = range(8)
SOURCE, PASS, USE, NOTHING = 8, 12, 20, 31
LOW = (65510, 17936, 768, 0, 56448, 16576, 32, 258, 50190, 21507, 2, 138, 35562, 96, 1, 32808)
HIGH = (2056, 24555, 80, 8456, 45312, 55564, 84, 12352, 6272, 20652, 4613, 1, 0, 3178, 1600, 64)
STEPS = (
    (134254752, 205004962, 206102787, 83952264, 19063174, 78385680, 42222891, 46516932, 151407654, 89223593, 118348468, 114396434, 154412520, 120353508, 179939914, 221613459, 223751147, 247274802, 124582902, 187989104, 255618386, 192216434, 65535475, 65523615),
    (134254752, 205004962, 206102787, 83952264, 19063174, 78320140, 42108843, 52825028, 44258074, 208065736, 109748911, 30301239, 219063062, 210918859, 177383013, 225864806, 189617897, 114013531, 259964152, 183761516, 181643981, 251394797, 65534830, 65523615),
    (134254752, 205004962, 206102787, 13173380, 77914503, 80103579, 208591271, 145082308, 150048018, 213458097, 52004911, 117033484, 109780274, 117807118, 187985363, 190089869, 255622643, 169650764, 114015576, 181644239, 251394668, 249273005, 179534960, 65534701),
    (134254752, 205004962, 206102787, 13173380, 77848967, 80037527, 208013351, 145627204, 52714415, 46375878, 111899364, 114013158, 183749906, 185863571, 179522060, 124574897, 247163726, 251386412, 122469230, 253504721, 255617612, 192212306, 259849586, 65534572),
    (134254752, 205004962, 206102787, 140608132, 14930469, 50602647, 100194342, 118346692, 25398675, 92637766, 107819621, 97639910, 166103350, 44266455, 106146896, 236710714, 253618764, 52718062, 190102363, 111902195, 257735276, 179526833, 187988717, 65535217),
    (134254752, 205004962, 206102787, 140608132, 76288656, 145097619, 108581659, 124654532, 54823823, 210060998, 185869285, 105764838, 235243322, 251987559, 52719059, 190094126, 259845071, 111893036, 120356210, 179530574, 177421295, 249395053, 245050577, 65535217),
    (134254752, 205004962, 206102787, 13189637, 75768199, 82417688, 40989112, 52716059, 210559942, 214168251, 44256231, 185493553, 42146735, 109788272, 191211918, 54831311, 259845335, 255613613, 179526962, 233548364, 247167926, 190098254, 249281132, 65535346),
    (134254752, 205004962, 206102787, 13189637, 80290183, 32600487, 50602519, 118236102, 117010991, 216462099, 46466574, 124570769, 166402862, 102984628, 164895893, 54832214, 177421295, 175913838, 259849307, 187520721, 255614258, 179534444, 257731922, 65534701),
    (134254752, 205004962, 206102787, 140608132, 25285284, 92906004, 109699811, 50596751, 101009094, 99496676, 41526199, 159828750, 176583569, 124606893, 113674542, 245050319, 179530832, 120347954, 181648367, 253504979, 190102253, 259849070, 257731793, 65535217),
    (134254752, 205004962, 206102787, 140608132, 33673892, 101294616, 118088419, 42143123, 92693265, 107819748, 33137595, 216434967, 99879565, 122465335, 119899953, 253504076, 114011603, 183753389, 188426450, 255621722, 251395571, 164980466, 247168342, 65534830),
    (134254752, 205004962, 206102787, 13173380, 80306567, 34681255, 118235800, 213459910, 42143123, 52720614, 124590508, 54823823, 120343181, 116124752, 159620402, 253504022, 191715027, 190094126, 183758033, 238877292, 259964146, 250963695, 247163726, 65534830),
    (134254752, 205004962, 206102787, 13173380, 80306567, 26292647, 109781652, 213459910, 217680783, 100879376, 116120597, 177409427, 52710158, 54827693, 183754163, 114014828, 122465360, 120351437, 181648367, 190102640, 249394926, 187985363, 257736179, 65535217),
    (134254752, 205004962, 206102787, 140608005, 76223116, 145032079, 80087952, 208407181, 109699631, 46373943, 211379782, 177330861, 38639462, 245052314, 183757904, 40676045, 36936987, 247163673, 253500851, 173784047, 120355674, 192216434, 255618257, 65535475),
    (134254752, 205004962, 206102787, 140608005, 76288656, 144985095, 144233241, 54828071, 168117958, 120353381, 41528391, 26122523, 46379924, 96213548, 124582965, 48491729, 255618386, 179535218, 114006959, 247163468, 181644755, 245050319, 259849070, 65534959),
    (134254752, 205004962, 206102787, 13189637, 80290183, 143749543, 52758668, 150051372, 48493157, 50606866, 100889498, 120347669, 115788207, 177413426, 108288685, 190098619, 48002574, 185875700, 257731535, 114010829, 236714733, 192216183, 249277262, 65535475),
    (134254752, 205004962, 206102787, 13189637, 75702663, 82417172, 32600500, 44261911, 212591558, 214151735, 216418454, 111897164, 113674542, 50608748, 183392463, 179526704, 181640498, 247156115, 234118579, 232045529, 255621978, 257731664, 253163603, 65535475),
)


def pick(table, role):
    value = jnp.int32(table[0])
    for index in range(1, len(table)):
        value = jnp.where(role == index, jnp.int32(table[index]), value)
    return value


def kernel(
    solved, factor, dinv, features, covariance, acc,
    sv, fv, dv, fe, res, own, sib_out, sib_in, red_out, red_in, panels,
    load_sem, sv_sem, sib_s, sib_r, red_s, red_r, gat_s, gat_r, tree_s, tree_r,
):
    row = lax.axis_index("row")
    col = lax.axis_index("col")
    y, z = row // 4, row % 4
    x, core = col // 2, col % 2

    def at(xx, yy, zz, cc):
        return {"row": ((yy + 4) % 4) * 4 + (zz + 4) % 4, "col": ((xx + 4) % 4) * 2 + cc}

    sibling = at(x, y, z, 1 - core)
    along = (at(x + 1, y, z, core), at(x - 1, y, z, core), at(x + 2, y, z, core))
    around = (at(x, y + 1, z, core), at(x, y - 1, z, core), at(x, y, z + 1, core), at(x, y, z - 1, core))

    role = ((y - x + 4) % 4) * 4 + (z - 2 * core + 4) % 4
    low, high = pick(LOW, role), pick(HIGH, role)

    def remote(src, dst, send, recv, device):
        return pltpu.make_async_remote_copy(
            src_ref=src, dst_ref=dst, send_sem=send, recv_sem=recv, device_id=device, device_id_type=MESH
        )

    def frames_of(place):
        chip = (x + place % 4) % 4
        half = core if place < 4 else 1 - core
        return pl.multiple_of(chip * 256 + half * 128, 128)

    def sv_load(place):
        return pltpu.make_async_copy(
            solved.at[:, pl.ds(frames_of(place), 128)], sv.at[:, pl.ds(place * 128, 128)], sv_sem.at[place]
        )

    fv_load = pltpu.make_async_copy(factor.at[pl.ds(0, KB)], fv.at[pl.ds(0, KB)], load_sem.at[0])
    fv_rest = pltpu.make_async_copy(factor.at[pl.ds(KB, 3 * KB)], fv.at[pl.ds(KB, 3 * KB)], load_sem.at[1])
    fe_load = pltpu.make_async_copy(features.at[pl.ds(frames_of(0), 128)], fe, load_sem.at[2])
    dv_load = pltpu.make_async_copy(dinv, dv, load_sem.at[3])
    acc_load = pltpu.make_async_copy(covariance, acc, load_sem.at[4])

    fv_load.start()
    for place in (4, 5, 6, 7, 0, 1, 2, 3):
        sv_load(place).start()
    fv_rest.start()
    fe_load.start()
    dv_load.start()
    acc_load.start()

    barrier = pltpu.get_barrier_semaphore()
    for device in (sibling,) + along + around:
        pl.semaphore_signal(barrier, inc=1, device_id=device, device_id_type=MESH)

    def rows_of(k):
        return pl.ds(pl.multiple_of(k * KB, KB), KB)

    def sib_copy(k):
        return remote(sib_out.at[k], sib_in.at[k], sib_s.at[k], sib_r.at[k], sibling)

    def red_copy(k, m):
        return remote(red_out.at[k, m], red_in.at[k, m], red_s.at[k, m], red_r.at[k, m], along[m])

    def part_sibling(k):
        sib_out[k] = jnp.dot(fv[rows_of(k), :], sv[:, 512:], preferred_element_type=F32).astype(BF16)
        sib_copy(k).start()

    def part_own(k):
        own[k] = jnp.dot(fv[rows_of(k), :], sv[:, :512], preferred_element_type=F32)

    def reduce(k):
        sib_copy(k).wait_recv()
        for m, first in ((2, 256), (0, 128), (1, 384)):
            piece_cols = pl.ds(first, 128)
            red_out[k, m] = (own[k, :, piece_cols] + sib_in[k, :, piece_cols].astype(F32)).astype(BF16)
            red_copy(k, m).start()
        own[k, :, :128] = own[k, :, :128] + sib_in[k, :, :128].astype(F32)

    def piece(k, chip, half):
        return panels.at[k, 8 + (chip + 4) % 4, pl.ds(pl.multiple_of(half * 128, 128), 128)]

    def gather_copy(k, m):
        chip = (x, x, x, None, x, x - 1, x + 1, x + 2)[m]
        ref = piece(k, chip, core)
        return remote(ref, ref, gat_s.at[k, m], gat_r.at[k, m], along[m] if m < 3 else sibling)

    def make_panel(k):
        @pl.when(k == 0)
        def _():
            fe_load.wait()
            dv_load.wait()
            acc_load.wait()

        for m in range(3):
            red_copy(k, m).wait_recv()
        summed = own[k, :, :128] + red_in[k, 0].astype(F32) + red_in[k, 1].astype(F32) + red_in[k, 2].astype(F32)
        cols = pl.ds(pl.multiple_of(k * KB, KB), KB)
        res[:, cols] = (fe[:, cols].astype(F32) - summed.T).astype(BF16)
        panel = lax.dot_general(res[...], dv[rows_of(k), :], NT, preferred_element_type=F32)
        panels[k, 8 + x, pl.ds(pl.multiple_of(core * 128, 128), 128)] = panel.astype(BF16)
        for m in (4, 0, 1, 2):
            gather_copy(k, m).start()

    def from_along(m):
        def stage(k):
            gather_copy(k, m).wait_recv()
            gather_copy(k, m + 5).start()
        return stage

    def row_done(k):
        for m in range(4, 8):
            gather_copy(k, m).wait_recv()

    def tree_copy(k, u, d, src):
        return remote(panels.at[k, src], panels.at[k, u], tree_s.at[k, u, d], tree_r.at[k, u], around[d])

    def place_of(u):
        return jnp.where(u // 4 == role, 8 + (x + u % 4) % 4, u)

    def passes(u, d):
        word = jnp.where(u < 4, low, high)
        return (lax.shift_right_logical(word, (u % 4) * 4 + d) & 1) == 1

    def hand_on(k, u):
        for d in range(4):
            @pl.when(passes(u, d))
            def _():
                tree_copy(k, u, d, place_of(u)).start()

    def use(k, u):
        first = pl.multiple_of((u // 4) * 1024 + ((x + u % 4) % 4) * 256, 256)
        rows = panels[k, 8:12].reshape(1024, KB)
        acc[:, pl.ds(first, 256)] += lax.dot_general(
            rows, panels[k, place_of(u)], NT, preferred_element_type=F32
        )

    words = tuple(pick([line[index] for line in STEPS], role) for index in range(len(STEPS[0])))
    res[...] = jnp.zeros_like(res)
    fv_load.wait()
    for place in (4, 5, 6, 7):
        sv_load(place).wait()
    pl.semaphore_wait(barrier, 8)
    part_sibling(0)
    for place in (0, 1, 2, 3):
        sv_load(place).wait()
    part_own(0)
    fv_rest.wait()

    stages = (
        part_sibling, part_own, reduce, make_panel, from_along(0), from_along(1), from_along(2), row_done,
    )

    def step(place, word):
        code = lax.shift_right_logical(word, 7 * place) & 127
        k, kind = code // 32, code % 32

        @pl.when(jnp.logical_and(kind >= USE, kind < NOTHING))
        def _():
            use(k, kind - USE)

        @pl.when(jnp.logical_and(kind >= PASS, kind < USE))
        def _():
            tree_copy(k, kind - PASS, 0, kind - PASS).wait_recv()
            hand_on(k, kind - PASS)

        @pl.when(kind < PASS)
        def _():
            for index, stage in enumerate(stages):
                @pl.when(kind == index)
                def _():
                    stage(k)

            for j, m in enumerate((4, 6, 7, 5)):
                @pl.when(kind == SOURCE + j)
                def _():
                    gather_copy(k, m).wait_recv()
                    hand_on(k, role * 4 + j)

        return word

    def four_steps(_, line):
        lax.fori_loop(0, 4, step, line[0])
        return line[1:] + line[:1]

    lax.fori_loop(0, len(words), four_steps, words)

    @pl.loop(0, CHUNKS * 8)
    def _(t):
        k, u = t // 8, t % 8
        for d in range(4):
            @pl.when(passes(u, d))
            def _():
                tree_copy(k, u, d, u).wait_send()

    @pl.loop(0, CHUNKS)
    def _(k):
        sib_copy(k).wait_send()
        for m in range(3):
            red_copy(k, m).wait_send()
        for m in (0, 1, 2, 4, 5, 6, 7):
            gather_copy(k, m).wait_send()


def body(solved, factor_rows, diag_inverse, features, covariance):
    any_place = pl.BlockSpec(memory_space=pl.ANY)
    dma = pltpu.SemaphoreType.DMA
    return pl.pallas_call(
        kernel,
        out_shape=pltpu.VMEM((1024, 2048), F32),
        in_specs=[any_place] * 5,
        out_specs=pl.BlockSpec(memory_space=pltpu.VMEM),
        scratch_shapes=[
            pltpu.VMEM((1024, 1024), BF16),
            pltpu.VMEM((1024, 1024), BF16),
            pltpu.VMEM((1024, 1024), BF16),
            pltpu.VMEM((128, 1024), BF16),
            pltpu.VMEM((128, 1024), BF16),
            pltpu.VMEM((CHUNKS, KB, 512), F32),
            pltpu.VMEM((CHUNKS, KB, 512), BF16),
            pltpu.VMEM((CHUNKS, KB, 512), BF16),
            pltpu.VMEM((CHUNKS, 3, KB, 128), BF16),
            pltpu.VMEM((CHUNKS, 3, KB, 128), BF16),
            pltpu.VMEM((CHUNKS, 12, 256, KB), BF16),
            dma((5,)),
            dma((8,)),
            dma((CHUNKS,)),
            dma((CHUNKS,)),
            dma((CHUNKS, 3)),
            dma((CHUNKS, 3)),
            dma((CHUNKS, 8)),
            dma((CHUNKS, 8)),
            dma((CHUNKS, 8, 4)),
            dma((CHUNKS, 8)),
        ],
        compiler_params=pltpu.CompilerParams(
            collective_id=0, has_side_effects=True, vmem_limit_bytes=44 * 2**20
        ),
        cost_estimate=pl.CostEstimate(flops=7 * 10**9, bytes_accessed=24 * 10**6, transcendentals=0),
    )(solved, factor_rows, diag_inverse, features, covariance)


def solution(mesh):
    placed = (P("col", "row"), P(None, "col"), P(), P("row", None), P("row", "col"))
    return jax.shard_map(
        body, mesh=mesh, in_specs=placed, out_specs=P("row", "col"), check_vma=False
    )
```

time: 211 us -> 71.9 us (0.34)
  the two profiles are of different devices: /device:TPU:1 before, /device:TPU:68 now
where the time goes in v2:
time: 71.9 us; the launch traced here: 71.8 us
  Pallas kernels  68.4 us (95%)
  local copies, waits for them, and re-layouts  3.4 us (5%)
    pallas_call x1, Pallas kernels, body(): pl.pallas_call(kernel, out_shape=pltpu.VMEM((1024, 2048), F32), in_specs=...  68.4 us
    unnamed x1, local copies, waits for them, and re-layouts  3.4 us

profile of v2, /device:TPU:68, one launch (start us, length us, event | category | flops | bytes accessed | tf_op | source)
XLA Modules:
  0.0 71.8 jit_solution(5963945824249120063)
XLA Ops:
  0.0 68.4 %shard_map.55 = f32[1024,2048]{1,0:T(8,128)S(1)} custom-call(bf16[1024,1024]{1,0:T(8,128)(2,1)} %solved.1, bf16[1024,1024]{1,0:T(8,128)(2,1)} %factor.1, bf16[1024,1024]{1,0:T(8,128)(2,1)} %dinv.1, bf16[1024,1024]{1,0:T(8,128)(2,1)} %features.1, f32[1024,2048]{1,0:T(8,128)} %covariance.1), custom_call_target="tpu_custom_call" | custom-call | flops 7000000000 | bytes 24000000 | tf_op jit(solution)/shard_map/pallas_call | solution.py:253
  68.4 3.4 %copy.7 = f32[1024,2048]{1,0:T(8,128)} copy(f32[1024,2048]{1,0:T(8,128)S(1)} %shard_map.55) | data formatting | bytes 16777216

commit v3 on v2

v3 whole, which is shorter than its diff:
```python
import jax
import jax.numpy as jnp
from jax import lax
from jax.experimental import pallas as pl
from jax.experimental.pallas import tpu as pltpu
from jax.sharding import PartitionSpec as P

F32 = jnp.float32
BF16 = jnp.bfloat16
CHUNKS = 4
KB = 256
NT = (((1,), (1,)), ((), ()))
MESH = pl.DeviceIdType.MESH

(
    PART_SIBLING, PART_OWN, REDUCE, PANEL, FROM_PREV, FROM_NEXT, FROM_OPPOSITE, ROW_DONE,
) = range(8)
SOURCE, PASS, USE, DRAIN, OTHERS, NOTHING = 8, 12, 20, 28, 30, 31
MASKS = (
    (3994502, 32776, 3470214, 32776, 3994502, 32776, 3994502, 32776),
    (1073216, 1373067, 1074240, 1373067, 1073216, 1373067, 1073216, 1373067),
    (12288, 320, 12416, 320, 12288, 320, 12288, 320),
    (0, 528392, 0, 528392, 0, 528392, 0, 528392),
    (3457536, 2887680, 7651840, 2887680, 3457536, 2887680, 3457536, 2887680),
    (1049344, 3444748, 1050368, 3444748, 1049344, 3444748, 1049348, 3444748),
    (128, 324, 128, 324, 128, 324, 128, 324),
    (4098, 786688, 4098, 786688, 4098, 786688, 4198402, 786688),
    (3162126, 295424, 3162126, 295424, 3162126, 295424, 3162126, 295424),
    (1327107, 1311372, 1327107, 1311372, 1327107, 1311372, 1327107, 1311372),
    (2, 270341, 2, 270341, 2, 270341, 0, 270341),
    (522, 1, 522, 1, 522, 1, 522, 1),
    (2139018, 0, 2138762, 0, 2106250, 0, 41866, 0),
    (384, 49546, 0, 49546, 384, 49546, 384, 49546),
    (1, 24832, 1, 24832, 16385, 24832, 1, 24832),
    (2097288, 256, 2097288, 256, 2097288, 256, 2097288, 256),
)
STEPS = (
    (134254752, 205004962, 74485507, 84029758, 198231179, 21682192, 46418580, 53103639, 90157512, 112004370, 219342006, 118351153, 225798713, 222619753, 185985819, 122469108, 125065718, 253508569, 255618386, 192216434, 258947484, 65535580, 65523615, 65523615, 65523615, 65523615),
    (134254752, 205004962, 74485507, 84029758, 198231179, 21681676, 48483348, 27938073, 208801173, 111122346, 153996046, 156120139, 111893817, 161150139, 97924436, 162966710, 167652821, 259964119, 181647980, 127793052, 249281261, 65535580, 65523615, 65523615, 65523615, 65523615),
    (134254752, 205004962, 74485507, 15003966, 53971139, 265869723, 124160295, 34360207, 105800600, 25958330, 30274452, 118298134, 192212177, 190089869, 259849457, 177421682, 183753518, 164326480, 251390773, 253508462, 179534444, 246363804, 65535580, 65523615, 65523615, 65523615),
    (134254752, 205004962, 74485507, 14938430, 44265283, 101058583, 99221347, 52714551, 149637902, 38639413, 179532698, 56945615, 42150734, 120355823, 124582637, 109784144, 122469230, 253504721, 190102769, 257732051, 241642060, 245046907, 65535580, 65523615, 65523615, 65523615),
    (134254752, 205004962, 74485507, 8483134, 79143302, 48351140, 145098790, 265023920, 142968595, 147705255, 93194764, 98120372, 124625843, 166103398, 216352471, 185871182, 251387186, 249277907, 252082193, 190097996, 242948781, 104644084, 179535161, 171800220, 127826137, 65535580),
    (134254752, 205004962, 74485507, 8483134, 35103110, 40441893, 57248775, 32305605, 54823934, 124654532, 168117958, 185725541, 36483887, 46373785, 192535891, 251987568, 110401070, 166423862, 181644213, 259841201, 251395442, 163293772, 187988821, 237452013, 245046905, 65535580),
    (134254752, 205004962, 74485507, 8483134, 140624677, 75902736, 118084400, 146780563, 143018139, 124576710, 48493157, 44266470, 120351824, 42146735, 109784531, 253496078, 94678225, 183753370, 259849457, 251387186, 162732846, 190098132, 246789838, 228439836, 127842676, 65535580),
    (134254752, 205004962, 74485507, 8483134, 140624677, 82416222, 146328463, 143001726, 118609990, 211377071, 217681299, 46369292, 114003089, 109780403, 44264399, 181644368, 251387057, 192204050, 249277004, 111901808, 255618257, 259841330, 190102124, 257259853, 127760028, 65535580),
    (134254752, 205004962, 74485507, 10563902, 77046150, 142803877, 208343828, 145082366, 33774119, 101059270, 100217528, 214279054, 95276177, 216451509, 124578380, 54827822, 183757517, 245046449, 122465360, 251390798, 192215789, 190098641, 253508462, 241646833, 257728123, 65535580),
    (134254752, 205004962, 74485507, 10563902, 77046150, 142869413, 208409368, 36784638, 117887897, 92611340, 108606132, 49399739, 27702034, 120353685, 122542383, 184920078, 192227788, 253504721, 114120366, 183757517, 190102769, 164051564, 230615923, 251492719, 249273978, 65535580),
    (134254752, 205004962, 74485507, 10563902, 140624676, 82416350, 145833827, 101813264, 56941639, 217690725, 109775372, 124148113, 48483602, 103533197, 122461367, 168512270, 175320117, 190098900, 170638448, 238283958, 179535063, 227786098, 230488662, 251395573, 248461084, 65535580),
    (134254752, 205004962, 74485507, 10563902, 140624676, 82416350, 145833827, 93424140, 209967687, 50606743, 44266470, 116120624, 56937617, 177412781, 54823694, 183753518, 179526833, 245046707, 169565490, 186379086, 187988981, 173468144, 238795866, 259849462, 256850204, 65535580),
    (134254752, 205004962, 74485507, 8483134, 26714502, 32052773, 34685837, 48583444, 102729571, 50973508, 111895348, 213070392, 96774727, 99463962, 217406413, 185985103, 122468972, 52718414, 250017683, 253508333, 125089587, 239893338, 187989305, 237448659, 259849404, 65535580),
    (134254752, 205004962, 74485507, 8483134, 35103110, 36247589, 53562375, 39825830, 118088218, 103910029, 213461049, 105180231, 30323483, 170232332, 187504231, 252631536, 49498066, 255618389, 99335538, 177413046, 175860558, 111901403, 232467407, 259849076, 250558364, 65535580),
    (134254752, 205004962, 74485507, 8483134, 140624677, 82416222, 265373923, 43058713, 110220870, 213454098, 45713293, 34360295, 118234264, 56941874, 188033228, 190094771, 46917262, 167537335, 228375767, 97921140, 192216374, 111901421, 234077296, 249281494, 127859100, 65535580),
    (134254752, 205004962, 74485507, 8483134, 140624677, 43487756, 109695788, 146780559, 45155991, 46375878, 52720229, 216888109, 54831692, 116120366, 51599504, 101968569, 227449906, 56949335, 247164113, 190102382, 251387315, 257735921, 185871827, 165558300, 259841622, 65535580),
)


def pick(table, role):
    value = jnp.asarray(table[0], jnp.int32)
    for index in range(1, len(table)):
        value = jnp.where(role == index, jnp.asarray(table[index], jnp.int32), value)
    return value


def kernel(
    solved, factor, dinv, features, covariance, acc,
    sv, fv, dv, fe, res, own, sib_out, sib_in, red_out, red_in, panels,
    load_sem, sv_sem, sib_s, sib_r, red_s, red_r, gat_s, gat_r, tree_s, tree_r,
):
    row = lax.axis_index("row")
    col = lax.axis_index("col")
    y, z = row // 4, row % 4
    x, core = col // 2, col % 2

    def at(xx, yy, zz, cc):
        return {"row": ((yy + 4) % 4) * 4 + (zz + 4) % 4, "col": ((xx + 4) % 4) * 2 + cc}

    sibling = at(x, y, z, 1 - core)
    along = (at(x + 1, y, z, core), at(x - 1, y, z, core), at(x + 2, y, z, core))
    around = (
        at(x, y + 1, z, core), at(x, y - 1, z, core), at(x, y, z + 1, core), at(x, y, z - 1, core),
        at(x, y + 2, z, core), at(x, y, z + 2, core),
    )

    ahead = (y - x + 4) % 4
    role = ahead * 4 + (z - 2 * core + 4) % 4
    masks = [pick([line[index] for line in MASKS], role) for index in range(2 * CHUNKS)]

    def remote(src, dst, send, recv, device):
        return pltpu.make_async_remote_copy(
            src_ref=src, dst_ref=dst, send_sem=send, recv_sem=recv, device_id=device, device_id_type=MESH
        )

    def frames_of(place):
        chip = (x + place % 4) % 4
        half = core if place < 4 else 1 - core
        return pl.multiple_of(chip * 256 + half * 128, 128)

    def sv_load(place):
        return pltpu.make_async_copy(
            solved.at[:, pl.ds(frames_of(place), 128)], sv.at[:, pl.ds(place * 128, 128)], sv_sem.at[place]
        )

    fv_load = pltpu.make_async_copy(factor.at[pl.ds(0, KB)], fv.at[pl.ds(0, KB)], load_sem.at[0])
    fv_rest = pltpu.make_async_copy(factor.at[pl.ds(KB, 3 * KB)], fv.at[pl.ds(KB, 3 * KB)], load_sem.at[1])
    fe_load = pltpu.make_async_copy(features.at[pl.ds(frames_of(0), 128)], fe, load_sem.at[2])
    dv_load = pltpu.make_async_copy(dinv, dv, load_sem.at[3])
    acc_load = pltpu.make_async_copy(covariance, acc, load_sem.at[4])

    fv_load.start()
    for place in (4, 5, 6, 7, 0, 1, 2, 3):
        sv_load(place).start()
    fv_rest.start()
    fe_load.start()
    dv_load.start()
    acc_load.start()

    barrier = pltpu.get_barrier_semaphore()
    for device in (sibling,) + along + around:
        pl.semaphore_signal(barrier, inc=1, device_id=device, device_id_type=MESH)

    def rows_of(k):
        return pl.ds(pl.multiple_of(k * KB, KB), KB)

    def sib_copy(k):
        return remote(sib_out.at[k], sib_in.at[k], sib_s.at[k], sib_r.at[k], sibling)

    def red_copy(k, m):
        return remote(red_out.at[k, m], red_in.at[k, m], red_s.at[k, m], red_r.at[k, m], along[m])

    def part_sibling(k, ready=lambda: None):
        sib_out[k] = jnp.dot(fv[rows_of(k), :], sv[:, 512:], preferred_element_type=F32).astype(BF16)
        ready()
        sib_copy(k).start()

    def part_own(k):
        own[k] = jnp.dot(fv[rows_of(k), :], sv[:, :512], preferred_element_type=F32)

    def reduce(k):
        sib_copy(k).wait_recv()
        for m, first in ((2, 256), (0, 128), (1, 384)):
            piece_cols = pl.ds(first, 128)
            red_out[k, m] = (own[k, :, piece_cols] + sib_in[k, :, piece_cols].astype(F32)).astype(BF16)
            red_copy(k, m).start()
        own[k, :, :128] = own[k, :, :128] + sib_in[k, :, :128].astype(F32)

    def piece(k, chip, half):
        return panels.at[k, 8 + (chip + 4) % 4, pl.ds(pl.multiple_of(half * 128, 128), 128)]

    def gather_copy(k, m):
        chip = (x, x, x, None, x, x - 1, x + 1, x + 2)[m]
        ref = piece(k, chip, core)
        return remote(ref, ref, gat_s.at[k, m], gat_r.at[k, m], along[m] if m < 3 else sibling)

    def first_copy(k):
        ref = piece(k, x, core)
        slot = jnp.where(ahead == 1, 0, jnp.where(ahead == 3, 1, 2)) + jnp.where(core == z // 2, 0, 5)
        return remote(ref, ref, gat_s.at[k, 3], gat_r.at[k, slot], at(y, y, z, z // 2))

    def whole_copy(k, m):
        ref = panels.at[k, 8 + (x + (3, 1, 2)[m]) % 4]
        return remote(ref, ref, gat_s.at[k, m + 5], gat_r.at[k, m + 5], sibling)

    def others(k, do):
        for m, steps in enumerate((1, 3, 2)):
            @pl.when(ahead != steps)
            def _():
                do(gather_copy(k, m))

    def make_panel(k):
        @pl.when(k == 0)
        def _():
            fe_load.wait()
            dv_load.wait()
            acc_load.wait()

        for m in range(3):
            red_copy(k, m).wait_recv()
        summed = own[k, :, :128] + red_in[k, 0].astype(F32) + red_in[k, 1].astype(F32) + red_in[k, 2].astype(F32)
        cols = pl.ds(pl.multiple_of(k * KB, KB), KB)
        res[:, cols] = (fe[:, cols].astype(F32) - summed.T).astype(BF16)
        panel = lax.dot_general(res[...], dv[rows_of(k), :], NT, preferred_element_type=F32)
        panels[k, 8 + x, pl.ds(pl.multiple_of(core * 128, 128), 128)] = panel.astype(BF16)
        @pl.when(ahead != 0)
        def _():
            first_copy(k).start()

        gather_copy(k, 4).start()

    def from_along(m):
        def stage(k):
            gather_copy(k, m).wait_recv()
            gather_copy(k, m + 5).start()
        return stage

    def row_done(k):
        gather_copy(k, 4).wait_recv()

        @pl.when(ahead != 0)
        def _():
            for m in range(3):
                gather_copy(k, m + 5).wait_recv()

        @pl.when(ahead == 0)
        def _():
            for m in range(3):
                whole_copy(k, m).wait_recv()

    def tree_copy(k, u, d, src):
        return remote(panels.at[k, src], panels.at[k, u], tree_s.at[k, u, d], tree_r.at[k, u], around[d])

    def place_of(u):
        return jnp.where(u // 4 == role, 8 + (x + u % 4) % 4, u)

    def each_way(k, u, do):
        bits = lax.shift_right_logical(pick(masks, 2 * k + u // 4), (u % 4) * 6) & 63
        for d in range(6):
            @pl.when((lax.shift_right_logical(bits, d) & 1) == 1)
            def _():
                do(d)

    def hand_on(k, u):
        each_way(k, u, lambda d: tree_copy(k, u, d, place_of(u)).start())

    def drain(k):
        @pl.loop(0, 8)
        def _(u):
            each_way(k, u, lambda d: tree_copy(k, u, d, u).wait_send())

        sib_copy(k).wait_send()
        for m in range(3):
            red_copy(k, m).wait_send()
        gather_copy(k, 4).wait_send()
        others(k, lambda copy: copy.wait_send())

        @pl.when(ahead != 0)
        def _():
            first_copy(k).wait_send()
            for m in range(3):
                gather_copy(k, m + 5).wait_send()

        @pl.when(role < 2)
        def _():
            for m in range(3):
                whole_copy(k, m).wait_send()

    def use(k, u):
        first = pl.multiple_of((u // 4) * 1024 + ((x + u % 4) % 4) * 256, 256)
        rows = panels[k, 8:12].reshape(1024, KB)
        acc[:, pl.ds(first, 256)] += lax.dot_general(
            rows, panels[k, place_of(u)], NT, preferred_element_type=F32
        )

    words = tuple(pick([line[index] for line in STEPS], role) for index in range(len(STEPS[0])))
    res[...] = jnp.zeros_like(res)
    fv_load.wait()
    for place in (4, 5, 6, 7):
        sv_load(place).wait()
    for place in (0, 1, 2, 3):
        sv_load(place).wait()
    part_own(0)
    part_sibling(0, lambda: pl.semaphore_wait(barrier, 10))
    fv_rest.wait()

    stages = (
        part_sibling, part_own, reduce, make_panel, from_along(0), from_along(1), from_along(2), row_done,
    )

    def step(place, word):
        code = lax.shift_right_logical(word, 7 * place) & 127
        k, kind = code // 32, code % 32

        @pl.when(jnp.logical_and(kind >= USE, kind < DRAIN))
        def _():
            use(k, kind - USE)

        @pl.when(jnp.logical_and(kind >= PASS, kind < USE))
        def _():
            tree_copy(k, kind - PASS, 0, kind - PASS).wait_recv()
            hand_on(k, kind - PASS)

        @pl.when(kind < PASS)
        def _():
            for index, stage in enumerate(stages):
                @pl.when(kind == index)
                def _():
                    stage(k)

            @pl.when(kind == SOURCE)
            def _():
                gather_copy(k, 4).wait_recv()
                hand_on(k, role * 4)

            for j, m in ((1, 1), (2, 2), (3, 0)):
                @pl.when(kind == SOURCE + j)
                def _():
                    gather_copy(k, m).wait_recv()
                    gather_copy(k, m + 5).wait_recv()
                    hand_on(k, role * 4 + j)
                    whole_copy(k, m).start()

        @pl.when(kind == DRAIN)
        def _():
            drain(k)

        @pl.when(kind == OTHERS)
        def _():
            others(k, lambda copy: copy.start())

        return word

    def four_steps(_, line):
        lax.fori_loop(0, 4, step, line[0])
        return line[1:] + line[:1]

    lax.fori_loop(0, len(words), four_steps, words)


def body(solved, factor_rows, diag_inverse, features, covariance):
    any_place = pl.BlockSpec(memory_space=pl.ANY)
    dma = pltpu.SemaphoreType.DMA
    return pl.pallas_call(
        kernel,
        out_shape=pltpu.VMEM((1024, 2048), F32),
        in_specs=[any_place] * 5,
        out_specs=pl.BlockSpec(memory_space=pltpu.VMEM),
        scratch_shapes=[
            pltpu.VMEM((1024, 1024), BF16),
            pltpu.VMEM((1024, 1024), BF16),
            pltpu.VMEM((1024, 1024), BF16),
            pltpu.VMEM((128, 1024), BF16),
            pltpu.VMEM((128, 1024), BF16),
            pltpu.VMEM((CHUNKS, KB, 512), F32),
            pltpu.VMEM((CHUNKS, KB, 512), BF16),
            pltpu.VMEM((CHUNKS, KB, 512), BF16),
            pltpu.VMEM((CHUNKS, 3, KB, 128), BF16),
            pltpu.VMEM((CHUNKS, 3, KB, 128), BF16),
            pltpu.VMEM((CHUNKS, 12, 256, KB), BF16),
            dma((5,)),
            dma((8,)),
            dma((CHUNKS,)),
            dma((CHUNKS,)),
            dma((CHUNKS, 3)),
            dma((CHUNKS, 3)),
            dma((CHUNKS, 8)),
            dma((CHUNKS, 8)),
            dma((CHUNKS, 8, 6)),
            dma((CHUNKS, 8)),
        ],
        compiler_params=pltpu.CompilerParams(
            collective_id=0, has_side_effects=True, vmem_limit_bytes=44 * 2**20
        ),
        cost_estimate=pl.CostEstimate(flops=7 * 10**9, bytes_accessed=24 * 10**6, transcendentals=0),
    )(solved, factor_rows, diag_inverse, features, covariance)


def solution(mesh):
    placed = (P("col", "row"), P(None, "col"), P(), P("row", None), P("row", "col"))
    return jax.shard_map(
        body, mesh=mesh, in_specs=placed, out_specs=P("row", "col"), check_vma=False
    )
```

time: 71.9 us -> 71.3 us (level)
  the two profiles are of different devices: /device:TPU:68 before, /device:TPU:1 now
where the time goes in v3:
time: 71.3 us; the launch traced here: 71.2 us
  Pallas kernels  67.8 us (95%)
  local copies, waits for them, and re-layouts  3.4 us (5%)
    pallas_call x1, Pallas kernels, body(): pl.pallas_call(kernel, out_shape=pltpu.VMEM((1024, 2048), F32), in_specs=...  67.8 us
    unnamed x1, local copies, waits for them, and re-layouts  3.4 us

profile of v3, /device:TPU:1, one launch (start us, length us, event | category | flops | bytes accessed | tf_op | source)
XLA Modules:
  0.0 71.2 jit_solution(309753374629446629)
XLA Ops:
  0.0 67.8 %shard_map.55 = f32[1024,2048]{1,0:T(8,128)S(1)} custom-call(bf16[1024,1024]{1,0:T(8,128)(2,1)} %solved.1, bf16[1024,1024]{1,0:T(8,128)(2,1)} %factor.1, bf16[1024,1024]{1,0:T(8,128)(2,1)} %dinv.1, bf16[1024,1024]{1,0:T(8,128)(2,1)} %features.1, f32[1024,2048]{1,0:T(8,128)} %covariance.1), custom_call_target="tpu_custom_call" | custom-call | flops 7000000000 | bytes 24000000 | tf_op jit(solution)/shard_map/pallas_call | solution.py:321
  67.8 3.4 %copy.7 = f32[1024,2048]{1,0:T(8,128)} copy(f32[1024,2048]{1,0:T(8,128)S(1)} %shard_map.55) | data formatting | bytes 16777216

commit v4 on v3

--- a/solution.py
+++ b/solution.py
@@ -17,40 +17,40 @@
 ) = range(8)
 SOURCE, PASS, USE, DRAIN, OTHERS, NOTHING = 8, 12, 20, 28, 30, 31
 MASKS = (
-    (3994502, 32776, 3470214, 32776, 3994502, 32776, 3994502, 32776),
-    (1073216, 1373067, 1074240, 1373067, 1073216, 1373067, 1073216, 1373067),
-    (12288, 320, 12416, 320, 12288, 320, 12288, 320),
-    (0, 528392, 0, 528392, 0, 528392, 0, 528392),
-    (3457536, 2887680, 7651840, 2887680, 3457536, 2887680, 3457536, 2887680),
-    (1049344, 3444748, 1050368, 3444748, 1049344, 3444748, 1049348, 3444748),
-    (128, 324, 128, 324, 128, 324, 128, 324),
-    (4098, 786688, 4098, 786688, 4098, 786688, 4198402, 786688),
-    (3162126, 295424, 3162126, 295424, 3162126, 295424, 3162126, 295424),
-    (1327107, 1311372, 1327107, 1311372, 1327107, 1311372, 1327107, 1311372),
-    (2, 270341, 2, 270341, 2, 270341, 0, 270341),
-    (522, 1, 522, 1, 522, 1, 522, 1),
-    (2139018, 0, 2138762, 0, 2106250, 0, 41866, 0),
-    (384, 49546, 0, 49546, 384, 49546, 384, 49546),
-    (1, 24832, 1, 24832, 16385, 24832, 1, 24832),
-    (2097288, 256, 2097288, 256, 2097288, 256, 2097288, 256),
+    (1597889, 137, 1847426, 2097155, 1348417, 529026, 2937731, 2920458),
+    (1597440, 2400655, 1048576, 2642507, 1597826, 1876615, 8258, 3191241),
+    (136, 16643, 524608, 24577, 1048640, 1310784, 2359300, 786560),
+    (262656, 2359360, 0, 2097160, 8192, 1573376, 2404480, 4096),
+    (589, 295040, 2113540, 40968, 2413069, 778, 20493, 1310729),
+    (2097156, 2359553, 16385, 2134849, 24578, 278540, 21314, 21257),
+    (33283, 4, 2363392, 384, 4675, 1048577, 385, 1057024),
+    (32899, 33025, 2629632, 32896, 2101321, 1048579, 4104, 262273),
+    (58117, 2105856, 33418, 2101248, 2379777, 128, 3149828, 512),
+    (1573120, 1368960, 132, 2654540, 524288, 2122496, 787264, 33541),
+    (1572992, 802880, 1048578, 540932, 8, 1069120, 0, 16386),
+    (45121, 4160, 8322, 524608, 65, 8197, 32768, 0),
+    (532740, 10, 2646414, 32776, 2097280, 41472, 2621448, 2097728),
+    (1589252, 2121864, 553413, 3670532, 1573504, 1089670, 16384, 541316),
+    (1048576, 1052674, 2118081, 1613824, 524288, 528384, 524289, 2646021),
+    (266240, 278528, 1, 513, 33289, 4224, 2097802, 16384),
 )
 STEPS = (
-    (134254752, 205004962, 74485507, 84029758, 198231179, 21682192, 46418580, 53103639, 90157512, 112004370, 219342006, 118351153, 225798713, 222619753, 185985819, 122469108, 125065718, 253508569, 255618386, 192216434, 258947484, 65535580, 65523615, 65523615, 65523615, 65523615),
-    (134254752, 205004962, 74485507, 84029758, 198231179, 21681676, 48483348, 27938073, 208801173, 111122346, 153996046, 156120139, 111893817, 161150139, 97924436, 162966710, 167652821, 259964119, 181647980, 127793052, 249281261, 65535580, 65523615, 65523615, 65523615, 65523615),
-    (134254752, 205004962, 74485507, 15003966, 53971139, 265869723, 124160295, 34360207, 105800600, 25958330, 30274452, 118298134, 192212177, 190089869, 259849457, 177421682, 183753518, 164326480, 251390773, 253508462, 179534444, 246363804, 65535580, 65523615, 65523615, 65523615),
-    (134254752, 205004962, 74485507, 14938430, 44265283, 101058583, 99221347, 52714551, 149637902, 38639413, 179532698, 56945615, 42150734, 120355823, 124582637, 109784144, 122469230, 253504721, 190102769, 257732051, 241642060, 245046907, 65535580, 65523615, 65523615, 65523615),
-    (134254752, 205004962, 74485507, 8483134, 79143302, 48351140, 145098790, 265023920, 142968595, 147705255, 93194764, 98120372, 124625843, 166103398, 216352471, 185871182, 251387186, 249277907, 252082193, 190097996, 242948781, 104644084, 179535161, 171800220, 127826137, 65535580),
-    (134254752, 205004962, 74485507, 8483134, 35103110, 40441893, 57248775, 32305605, 54823934, 124654532, 168117958, 185725541, 36483887, 46373785, 192535891, 251987568, 110401070, 166423862, 181644213, 259841201, 251395442, 163293772, 187988821, 237452013, 245046905, 65535580),
-    (134254752, 205004962, 74485507, 8483134, 140624677, 75902736, 118084400, 146780563, 143018139, 124576710, 48493157, 44266470, 120351824, 42146735, 109784531, 253496078, 94678225, 183753370, 259849457, 251387186, 162732846, 190098132, 246789838, 228439836, 127842676, 65535580),
-    (134254752, 205004962, 74485507, 8483134, 140624677, 82416222, 146328463, 143001726, 118609990, 211377071, 217681299, 46369292, 114003089, 109780403, 44264399, 181644368, 251387057, 192204050, 249277004, 111901808, 255618257, 259841330, 190102124, 257259853, 127760028, 65535580),
-    (134254752, 205004962, 74485507, 10563902, 77046150, 142803877, 208343828, 145082366, 33774119, 101059270, 100217528, 214279054, 95276177, 216451509, 124578380, 54827822, 183757517, 245046449, 122465360, 251390798, 192215789, 190098641, 253508462, 241646833, 257728123, 65535580),
-    (134254752, 205004962, 74485507, 10563902, 77046150, 142869413, 208409368, 36784638, 117887897, 92611340, 108606132, 49399739, 27702034, 120353685, 122542383, 184920078, 192227788, 253504721, 114120366, 183757517, 190102769, 164051564, 230615923, 251492719, 249273978, 65535580),
-    (134254752, 205004962, 74485507, 10563902, 140624676, 82416350, 145833827, 101813264, 56941639, 217690725, 109775372, 124148113, 48483602, 103533197, 122461367, 168512270, 175320117, 190098900, 170638448, 238283958, 179535063, 227786098, 230488662, 251395573, 248461084, 65535580),
-    (134254752, 205004962, 74485507, 10563902, 140624676, 82416350, 145833827, 93424140, 209967687, 50606743, 44266470, 116120624, 56937617, 177412781, 54823694, 183753518, 179526833, 245046707, 169565490, 186379086, 187988981, 173468144, 238795866, 259849462, 256850204, 65535580),
-    (134254752, 205004962, 74485507, 8483134, 26714502, 32052773, 34685837, 48583444, 102729571, 50973508, 111895348, 213070392, 96774727, 99463962, 217406413, 185985103, 122468972, 52718414, 250017683, 253508333, 125089587, 239893338, 187989305, 237448659, 259849404, 65535580),
-    (134254752, 205004962, 74485507, 8483134, 35103110, 36247589, 53562375, 39825830, 118088218, 103910029, 213461049, 105180231, 30323483, 170232332, 187504231, 252631536, 49498066, 255618389, 99335538, 177413046, 175860558, 111901403, 232467407, 259849076, 250558364, 65535580),
-    (134254752, 205004962, 74485507, 8483134, 140624677, 82416222, 265373923, 43058713, 110220870, 213454098, 45713293, 34360295, 118234264, 56941874, 188033228, 190094771, 46917262, 167537335, 228375767, 97921140, 192216374, 111901421, 234077296, 249281494, 127859100, 65535580),
-    (134254752, 205004962, 74485507, 8483134, 140624677, 43487756, 109695788, 146780559, 45155991, 46375878, 52720229, 216888109, 54831692, 116120366, 51599504, 101968569, 227449906, 56949335, 247164113, 190102382, 251387315, 257735921, 185871827, 165558300, 259841622, 65535580),
+    (134254752, 205004962, 17862403, 85499683, 100926603, 140823050, 90533704, 50713750, 54826267, 219732660, 156391934, 103671222, 177134776, 182086379, 244709482, 249392337, 253143415, 259845200, 257727794, 192203921, 60710513, 65535580, 65523615, 65523615, 65523615, 65523615),
+    (134254752, 205004962, 17862403, 85499683, 50496651, 198320527, 48941709, 57052329, 30301226, 265957782, 116122953, 185523531, 188406316, 223802586, 255732429, 183762426, 26556108, 249281172, 245045933, 181639982, 127782511, 65535580, 65523615, 65523615, 65523615, 65523615),
+    (134254752, 205004962, 74485507, 140783934, 265865438, 31869959, 105506839, 42174010, 100017046, 174921271, 241600859, 255622631, 119888013, 183757517, 118234547, 251390540, 249273005, 114015602, 245050577, 247163726, 253496723, 126299474, 65535580, 65523615, 65523615, 65523615),
+    (134254752, 205004962, 74485507, 198242622, 16757136, 35980824, 109777817, 124570253, 102065863, 164534584, 100398038, 175864759, 39566043, 248915994, 48495728, 166615249, 46381527, 41729497, 95632667, 190097973, 255613742, 126302828, 65535580, 65523615, 65523615, 65523615),
+    (134254752, 205004962, 74485507, 10694974, 197239172, 77923213, 101059216, 80284131, 99024716, 97325996, 143530934, 227812165, 149841585, 210545364, 122925925, 217442262, 233015512, 236784790, 54836343, 48495470, 190093997, 259849457, 187981235, 247168370, 127330716, 65535580),
+    (134254752, 205004962, 74485507, 10760510, 13681200, 16222604, 57021076, 80291939, 118085886, 52714674, 122774340, 109787212, 185920071, 215577134, 237227282, 114947607, 124579314, 181648500, 247168377, 116125010, 249273005, 179522189, 259845071, 251391185, 59082556, 65535580),
+    (134254752, 205004962, 74485507, 8483134, 75607875, 50451088, 81757795, 82928148, 104425542, 150581817, 159795416, 56947668, 174954287, 33320375, 257735831, 226721267, 244688661, 106260205, 108313274, 118238523, 252033038, 166411247, 112957108, 55855447, 126303065, 65535580),
+    (134254752, 205004962, 74485507, 8483134, 25276227, 42062500, 27901795, 51448464, 118232005, 36909766, 210622361, 109785927, 227944532, 244964529, 122464973, 181635854, 183761903, 174937838, 98416731, 48494774, 241600819, 259947579, 247168370, 187977107, 126299474, 65535580),
+    (134254752, 205004962, 74485507, 8483134, 25276227, 78187015, 265865260, 44258072, 82578319, 118579764, 30510225, 99010966, 159685604, 149648229, 97852058, 245046119, 181640627, 251387186, 187984847, 253504850, 232062193, 248966224, 256792818, 230619548, 127231733, 65535580),
+    (134254752, 205004962, 74485507, 8483134, 33664835, 78187527, 265865392, 40178444, 38391193, 118579738, 28412815, 120350741, 124901860, 123312485, 46379992, 173812945, 93027418, 255613620, 244771308, 163355438, 257272526, 230419407, 160168949, 241642039, 127776635, 65535580),
+    (134254752, 205004962, 74485507, 8483134, 14790467, 265867813, 101058598, 36577959, 26288921, 58296851, 38924901, 27641754, 184906704, 122461361, 30207185, 125576726, 95856980, 116128821, 191703468, 114015731, 257849586, 251394668, 181647004, 162916341, 127773422, 65535580),
+    (134254752, 205004962, 74485507, 8483134, 14790467, 26792485, 92607358, 147937831, 33900228, 211399320, 36822064, 159745817, 56947668, 111889682, 114002831, 124578896, 120355436, 251390669, 181640498, 173402012, 100513626, 246282477, 192686585, 187988344, 127860083, 65535580),
+    (134254752, 205004962, 74485507, 10563902, 14131628, 48351120, 44257956, 207820824, 29985406, 109696918, 111895236, 97623095, 211383862, 214885299, 216451567, 229948404, 246852172, 255622256, 104049873, 106179385, 185951930, 183762419, 54937873, 249277907, 126303602, 65535580),
+    (134254752, 205004962, 74485507, 8663358, 198236165, 50448518, 53154468, 33082642, 168153982, 82627213, 26026692, 47286036, 56944824, 211071675, 95841351, 189622758, 255457499, 115120302, 122469689, 183757517, 116128880, 259844684, 226966382, 127121396, 247167958, 65535580),
+    (134254752, 205004962, 74485507, 10563902, 33664835, 78187527, 81768880, 145822636, 117868852, 210094022, 185725648, 37329330, 42147097, 216976787, 116116238, 192207533, 114015731, 257735276, 251395313, 28601295, 182200085, 160742489, 247164244, 249273521, 126298829, 65535580),
+    (134254752, 205004962, 74485507, 10563902, 14790467, 34280100, 80101219, 145824295, 26319920, 116126228, 28943333, 216266261, 124582423, 251382929, 56985998, 173222734, 190126765, 245806738, 185440080, 104638961, 192309433, 232680141, 256809334, 259930608, 127264668, 65535580),
 )
 
 

time: 71.3 us -> 65.5 us (0.919)
  Pallas kernels: 67.8 us -> 61.5 us
    pallas_call x1, Pallas kernels: 67.8 us -> 61.5 us  [body(): pl.pallas_call(kernel, out_shape=pltpu.VMEM((1024, 2048), F32), in_specs=...]
where the time goes in v4:
time: 65.5 us; the launch traced here: 64.9 us
  Pallas kernels  61.5 us (94%)
  local copies, waits for them, and re-layouts  3.4 us (5%)
    pallas_call x1, Pallas kernels, body(): pl.pallas_call(kernel, out_shape=pltpu.VMEM((1024, 2048), F32), in_specs=...  61.5 us
    unnamed x1, local copies, waits for them, and re-layouts  3.4 us

profile of v4, /device:TPU:1, one launch (start us, length us, event | category | flops | bytes accessed | tf_op | source)
XLA Modules:
  0.0 64.9 jit_solution(9592777164894400585)
XLA Ops:
  0.0 61.5 %shard_map.55 = f32[1024,2048]{1,0:T(8,128)S(1)} custom-call(bf16[1024,1024]{1,0:T(8,128)(2,1)} %solved.1, bf16[1024,1024]{1,0:T(8,128)(2,1)} %factor.1, bf16[1024,1024]{1,0:T(8,128)(2,1)} %dinv.1, bf16[1024,1024]{1,0:T(8,128)(2,1)} %features.1, f32[1024,2048]{1,0:T(8,128)} %covariance.1), custom_call_target="tpu_custom_call" | custom-call | flops 7000000000 | bytes 24000000 | tf_op jit(solution)/shard_map/pallas_call | solution.py:321
  61.5 3.4 %copy.7 = f32[1024,2048]{1,0:T(8,128)} copy(f32[1024,2048]{1,0:T(8,128)S(1)} %shard_map.55) | data formatting | bytes 16777216

commit v5 on v4

--- a/solution.py
+++ b/solution.py
@@ -111,8 +111,6 @@
         sv_load(place).start()
     fv_rest.start()
     fe_load.start()
-    dv_load.start()
-    acc_load.start()
 
     barrier = pltpu.get_barrier_semaphore()
     for device in (sibling,) + along + around:
@@ -260,6 +258,8 @@
     part_own(0)
     part_sibling(0, lambda: pl.semaphore_wait(barrier, 10))
     fv_rest.wait()
+    dv_load.start()
+    acc_load.start()
 
     stages = (
         part_sibling, part_own, reduce, make_panel, from_along(0), from_along(1), from_along(2), row_done,

time: 65.5 us -> 65.4 us (level)
  no operation moved by 1% of the time
where the time goes in v5:
time: 65.4 us; the launch traced here: 65.3 us
  Pallas kernels  61.9 us (95%)
  local copies, waits for them, and re-layouts  3.4 us (5%)
    pallas_call x1, Pallas kernels, body(): pl.pallas_call(kernel, out_shape=pltpu.VMEM((1024, 2048), F32), in_specs=...  61.9 us
    unnamed x1, local copies, waits for them, and re-layouts  3.4 us

profile of v5, /device:TPU:1, one launch (start us, length us, event | category | flops | bytes accessed | tf_op | source)
XLA Modules:
  0.0 65.3 jit_solution(882710071925419210)
XLA Ops:
  0.0 61.9 %shard_map.55 = f32[1024,2048]{1,0:T(8,128)S(1)} custom-call(bf16[1024,1024]{1,0:T(8,128)(2,1)} %solved.1, bf16[1024,1024]{1,0:T(8,128)(2,1)} %factor.1, bf16[1024,1024]{1,0:T(8,128)(2,1)} %dinv.1, bf16[1024,1024]{1,0:T(8,128)(2,1)} %features.1, f32[1024,2048]{1,0:T(8,128)} %covariance.1), custom_call_target="tpu_custom_call" | custom-call | flops 7000000000 | bytes 24000000 | tf_op jit(solution)/shard_map/pallas_call | solution.py:321
  61.9 3.4 %copy.7 = f32[1024,2048]{1,0:T(8,128)} copy(f32[1024,2048]{1,0:T(8,128)S(1)} %shard_map.55) | data formatting | bytes 16777216
